TPU v7x, 32 devices: a whole 2x2x4 slice. The times are simulated.
32 devices in a mesh: groups: 2 (over y), row: 4 (over x, core), col: 4 (over z).
Axes of the slice: x: 2, y: 2, z: 4, core: 2. Of those that a mesh axis runs over, the one named last changes fastest.
Arguments:
- basis_values: bfloat16 [4, 4, 2048, 1536], P('row', 'col'), may hold values from -6 to 6
- potential: float32 [4, 4, 2048], P('row', 'col'), may hold values from -0.125 to 0.125
- basis_blocks: int32 [4, 4, 12], P('row', 'col'), may hold values from 0 to 63, as said below
- factor: bfloat16 [16, 4, 128, 1024], P(None, 'row', None, 'col'), may hold values from -0.1875 to 0.1875
Outputs:
- hamiltonian: float32 [32, 4, 16, 4, 128, 128], P('groups', 'row', None, 'col'), parts along dimension 0
- product: float32 [32, 4, 128, 16, 4, 128], P('groups', 'row', None, None, 'col'), parts along dimension 0
There are 2 independent parts, one for each index of `groups`. A program takes and returns all parts, laid end to end along the dimension named above; an argument that names none is the same for every part. Nothing has to cross between parts.
Inputs may be any that keep to these rules, and one draw needn't show every extreme that they name: `basis_blocks`: the 12 blocks of one batch are distinct and lie within 16 consecutive blocks counted cyclically over the 64 blocks of the window; every such range starts at one common offset modulo 16, and every block of the range whose position in it is a multiple of 4 is on the list. Hence at most 16 of a batch's block pairs (I, J) share the same (I mod 4, J mod 4), and some pair of residues has exactly 16.
All inputs are finite; a program needn't handle non-finite values.
Results may differ from a plain program's by a relative error of at most 0.0048.
Values may be sent and summed in bfloat16 or wider, within the bound.
A program may use at most 128 MiB of HBM per device.

v0:
```python
import jax
import jax.numpy as jnp
from jax import lax
from jax.sharding import PartitionSpec as P

NB = 8192
WIN = 16


def from_root(value, axis, source):
    kept = jnp.where(lax.axis_index(axis) == source, value, 0).astype(value.dtype)
    return lax.psum(kept, axis)


def slot_ranks(targets, usable):
    count = targets.shape[0]
    order = jnp.arange(count)
    earlier = order[None, :] < order[:, None]
    same_target = (targets[:, None] == targets[None, :]) & usable[None, :] & earlier
    return jnp.sum(same_target.astype(jnp.int32), axis=1)


def pack_slots(slot_of_item, slot_count, items, labels):
    selector = jnp.arange(slot_count)[:, None] == slot_of_item[None, :]
    packed = jnp.dot(
        selector.astype(jnp.bfloat16), items, preferred_element_type=jnp.float32
    ).astype(jnp.bfloat16)
    slot_labels = jnp.sum(jnp.where(selector, labels[None, :] + 1, 0), axis=1) - 1
    return (packed, slot_labels)


def sum_into_tile(received, received_labels, tile_blocks):
    selector = received_labels[:, None] == jnp.arange(tile_blocks)[None, :]
    return lax.dot_general(
        selector.astype(jnp.bfloat16),
        received,
        (((0,), (0,)), ((), ())),
        preferred_element_type=jnp.float32,
    )


def local(basis_values, potential, basis_blocks, factor):
    row_count = lax.axis_size("row")
    col_count = lax.axis_size("col")
    device_count = row_count * col_count
    phi_batch = basis_values[0, 0]
    weight_batch = potential[0, 0]
    block_list = basis_blocks[0, 0]
    list_length = block_list.shape[0]
    block_size = factor.shape[2]
    block_area = block_size * block_size
    window = WIN
    total_blocks = NB // block_size
    local_rows = total_blocks // row_count
    local_cols = total_blocks // col_count
    tile_blocks = local_rows * local_cols
    weighted = (phi_batch * weight_batch[:, None]).astype(jnp.bfloat16)
    partial_sum = lax.dot_general(
        phi_batch, weighted, (((0,), (0,)), ((), ())), preferred_element_type=jnp.float32
    ).astype(jnp.bfloat16)
    pieces = partial_sum.reshape(list_length, block_size, list_length, block_size).transpose(
        0, 2, 1, 3
    )
    row_share = min(list_length, window // row_count)
    col_share = min(list_length, window // col_count)
    row_label = jnp.broadcast_to(block_list[:, None], (list_length, list_length)).reshape(-1)
    col_label = jnp.broadcast_to(block_list[None, :], (list_length, list_length)).reshape(-1)
    owner = row_label % row_count * col_count + col_label % col_count
    capacity = row_share * col_share
    usable = jnp.ones(owner.shape, bool)
    slot_of_item = owner * capacity + slot_ranks(owner, usable)
    local_label = row_label // row_count * local_cols + col_label // col_count
    packed, slot_labels = pack_slots(
        slot_of_item,
        device_count * capacity,
        pieces.reshape(list_length * list_length, block_area),
        local_label,
    )
    packed = packed.reshape(device_count, capacity, block_area)
    slot_labels = slot_labels.reshape(device_count, capacity)
    received, received_labels = (
        lax.all_to_all(packed, ("row", "col"), split_axis=0, concat_axis=0, tiled=True),
        lax.all_to_all(slot_labels, ("row", "col"), split_axis=0, concat_axis=0, tiled=True),
    )
    tile = sum_into_tile(received.reshape(-1, block_area), received_labels.reshape(-1), tile_blocks)
    tile = tile.reshape(local_rows, local_cols, block_size, block_size)
    hamiltonian = tile.reshape(local_rows, 1, local_cols, 1, block_size, block_size)
    tile_narrow = tile.astype(jnp.bfloat16)
    head_width = factor.shape[3] * col_count
    head_blocks = head_width // block_size
    gathered_rows = []
    for block_row in range(head_blocks):
        gathered_rows.append(
            from_root(tile_narrow[block_row // row_count], "row", block_row % row_count)
        )
    head_stack = jnp.stack(gathered_rows, axis=0)
    head_matrix = head_stack.transpose(0, 2, 1, 3).reshape(head_width, local_cols * block_size)
    piece = lax.all_gather(factor, "col", axis=3, tiled=True)
    width = piece.shape[3]
    product = jnp.dot(
        piece.reshape(local_rows * block_size, width),
        head_matrix,
        preferred_element_type=jnp.float32,
    )
    product = product.reshape(local_rows, 1, block_size, local_cols, 1, block_size)
    return (hamiltonian, product)


def solution(mesh):
    return jax.shard_map(
        local,
        mesh=mesh,
        in_specs=(
            P("row", "col", None, None),
            P("row", "col", None),
            P("row", "col", None),
            P(None, "row", None, "col"),
        ),
        out_specs=(
            P("groups", "row", None, "col", None, None),
            P("groups", "row", None, None, "col", None),
        ),
        check_vma=False,
    )
```

profile of v0, /device:TPU:0, one launch (start us, length us, event | category | flops | bytes accessed | tf_op | source)
XLA Modules:
  0.0 423.9 jit_solution(7756939959881441454)
XLA Ops:
  8.0 0.7 broadcast_in_dim.45
  8.7 0.1 reshape.286
  8.7 0.7 broadcast_in_dim.44
  9.5 0.1 reshape.285
  9.6 0.2 convert_reduce_fusion
  9.8 0.1 select_reduce_fusion
  9.9 0.7 sub.19
  10.6 7.4 %all-to-all-start = ((s32[16,1,16]{2,1,0:T(1,128)}), s32[16,1,16]{2,1,0:T(1,128)S(1)}, u32[]{:S(2)}, u32[]{:S(2)}) async-start(s32[16,1,16]{2,1,0:T(1,128)} %sub.19), calls=%async_computation | async-start | bytes 16384 | tf_op jit(solution)/shard_map/all_to_all | solution.py:83
  18.0 15.6 %fusion = bf16[1536,1536]{0,1:T(8,128)(2,1)} fusion(bf16[1,1,2048,1536]{3,2,1,0:T(8,128)(2,1)} %param.4, f32[2048]{0:T(1024)} %bitcast.89), kind=kOutput, calls=%fused_computation.4 | convolution fusion | flops 9675472896 | bytes 11018240 | tf_op jit(solution)/shard_map/dot_general | solution.py:58
  33.6 6.6 %copy.20 = bf16[1536,1536]{1,0:T(8,128)(2,1)} copy(bf16[1536,1536]{0,1:T(8,128)(2,1)} %fusion) | data formatting | bytes 9437184 | tf_op jit(solution)/shard_map/convert_element_type | solution.py:60
  40.2 9.4 %reshape.287 = bf16[12,128,12,128]{3,2,1,0:T(8,128)(2,1)} reshape(bf16[1536,1536]{1,0:T(8,128)(2,1)} %copy.20) | data formatting | bytes 9437184 | tf_op jit(solution)/shard_map/reshape | solution.py:61
  49.6 4.1 copy.21
  53.8 7.4 %convolution_convert_fusion = bf16[256,16384]{1,0:T(8,128)(2,1)} fusion(bf16[18,8,128,128]{3,2,1,0:T(8,128)(2,1)S(1)} %bitcast.76, s32[144]{0:T(256)S(1)} %multiply_add_fusion), kind=kOutput, calls=%fused_computation | convolution fusion | flops 1212190720 | bytes 13107776 | tf_op jit(solution)/shard_map/dot_general | solution.py:25
  61.2 0.0 all-to-all-done
  61.2 6.1 %all-to-all-start.1 = ((bf16[16,16,16384]{2,1,0:T(8,128)(2,1)}), bf16[16,16,16384]{2,1,0:T(8,128)(2,1)}, u32[]{:S(2)}, u32[]{:S(2)}) async-start(bf16[16,16,16384]{2,1,0:T(8,128)(2,1)} %bitcast.74), calls=%async_computation.1 | async-start | bytes 16777216 | tf_op jit(solution)/shard_map/all_to_all | solution.py:82
  67.3 0.2 all-reduce.3.cloned.1.call-start
  67.5 0.5 broadcast.328
  68.0 0.7 reduce.3
  68.7 0.1 eq.66
  68.8 182.8 %all-to-all-done.1 = bf16[16,16,16384]{2,1,0:T(8,128)(2,1)} async-done(((bf16[16,16,16384]{2,1,0:T(8,128)(2,1)}), bf16[16,16,16384]{2,1,0:T(8,128)(2,1)}, u32[]{:S(2)}, u32[]{:S(2)}) %all-to-all-start.1) | async-done | bytes 8388640 | tf_op jit(solution)/shard_map/all_to_all | solution.py:82
  251.6 12.0 %fusion.17 = (bf16[256,16384]{1,0:T(8,128)(2,1)S(1)}, f32[256,16384]{1,0:T(8,128)}) fusion(bf16[256,16384]{1,0:T(8,128)(2,1)} %bitcast.7, s32[256]{0:T(256)S(1)} %eq.66), kind=kOutput, calls=%fused_computation.57 | convolution fusion | flops 2151743488 | bytes 33555456 | tf_op jit(solution)/shard_map/dot_general | solution.py:34
  263.6 0.3 select_bitcast_fusion
  263.9 0.1 copy.41
  264.0 1.2 copy.29
  265.1 0.1 copy.35
  265.2 1.2 copy.23
  266.4 0.1 copy.36
  266.5 1.1 copy.24
  267.6 0.1 copy.39
  267.7 1.1 copy.27
  268.9 0.1 copy.40
  269.0 1.1 copy.28
  270.1 0.1 copy.38
  270.2 1.2 copy.26
  271.3 0.1 copy.34
  271.4 1.2 copy.22
  272.6 0.1 copy.37
  272.7 1.1 copy.25
  273.8 0.0 all-reduce.3.cloned.1.call-update
  273.9 0.3 all-gather.2.cloned.1.call-start
  274.1 0.3 all-gather.2.cloned.1.call-update
  274.4 14.3 %copy.33 = f32[32,8,128,128]{3,2,1,0:T(8,128)} copy(f32[32,8,128,128]{3,1,2,0:T(8,128)} %bitcast.72) | data formatting | bytes 33554432
  288.8 70.7 %all-reduce.3.cloned.1.call-done = (bf16[1,16,128,128]{3,1,2,0:T(8,128)(2,1)}, bf16[1,16,128,128]{3,1,2,0:T(8,128)(2,1)}, bf16[1,16,128,128]{3,1,2,0:T(8,128)(2,...) async-done(((bf16[1,16,128,128]{3,1,2,0:T(8,128)(2,1)}, ...) | async-done | bytes 4194320 | tf_op jit(solution)/shard_map/psum | solution.py:12
  359.5 0.0 copy-start.2
  359.5 0.0 copy-start.1
  359.5 0.0 copy-start
  359.5 2.0 constant_dynamic-update-slice_fusion.7
  361.5 1.9 constant_dynamic-update-slice_fusion.6
  363.3 1.9 constant_dynamic-update-slice_fusion.5
  365.2 1.9 constant_dynamic-update-slice_fusion.4
  367.1 1.9 constant_dynamic-update-slice_fusion.3
  368.9 0.0 copy-done.2
  368.9 0.8 constant_dynamic-update-slice_fusion.2
  369.8 0.0 copy-done.1
  369.8 0.8 constant_dynamic-update-slice_fusion.1
  370.6 0.0 copy-done
  370.6 0.8 constant_dynamic-update-slice_fusion
  371.4 0.0 all-gather.2.cloned.1.call-done
  371.4 12.6 %convolution_bitcast_fusion = f32[256,8,16,128]{3,1,2,0:T(8,128)S(1)} fusion(bf16[2048,1024]{1,0:T(8,128)(2,1)} %bitcast.88, bf16[128,8,16,128]{3,2,1,0:T(8,128)(2,1)} %bitcast.44), kind=kOutput, calls=%fused_computation.2 | convolution fusion | flops 8589934592 | bytes 25165824 | tf_op jit(solution)/shard_map/dot_general | solution.py:100
  384.0 7.5 %copy.43 = f32[256,8,16,128]{3,2,1,0:T(8,128)} copy(f32[256,8,16,128]{3,1,2,0:T(8,128)S(1)} %convolution_bitcast_fusion) | data formatting | bytes 33554432
  391.5 24.9 %copy.31 = f32[16,1,128,16,1,128]{5,4,3,2,1,0:T(1,128)} copy(f32[16,1,128,16,1,128]{2,0,5,3,4,1:T(8,128)} %bitcast.73) | data formatting | bytes 33554432
  (3 shorter events, 0.0 us)
Async XLA Ops:
  10.6 50.6 %all-to-all-start = ((s32[16,1,16]{2,1,0:T(1,128)}), s32[16,1,16]{2,1,0:T(1,128)S(1)}, u32[]{:S(2)}, u32[]{:S(2)}) async-start(s32[16,1,16]{2,1,0:T(1,128)} %sub.19), calls=%async_computation | async-start | bytes 16384 | tf_op jit(solution)/shard_map/all_to_all | solution.py:83
  61.2 190.4 %all-to-all-start.1 = ((bf16[16,16,16384]{2,1,0:T(8,128)(2,1)}), bf16[16,16,16384]{2,1,0:T(8,128)(2,1)}, u32[]{:S(2)}, u32[]{:S(2)}) async-start(bf16[16,16,16384]{2,1,0:T(8,128)(2,1)} %bitcast.74), calls=%async_computation.1 | async-start | bytes 16777216 | tf_op jit(solution)/shard_map/all_to_all | solution.py:82
  67.3 292.2 %all-reduce.3.cloned.1.call-start = ((), (), s32[]{:S(2)}) async-start(), calls=%async_computation.3 | async-start | bytes 8388608 | tf_op jit(solution)/shard_map/psum | solution.py:12
  273.9 97.6 %all-gather.2.cloned.1.call-start = ((), (), s32[]{:S(2)}) async-start(), calls=%async_computation.2 | async-start | bytes 5242880 | tf_op jit(solution)/shard_map/all_gather | solution.py:98
  359.5 9.5 %copy-start.2 = (bf16[1,16,128,128]{3,1,2,0:T(8,128)(2,1)S(1)}, bf16[1,16,128,128]{3,1,2,0:T(8,128)(2,1)}, u32[]{:S(2)}) copy-start(bf16[1,16,128,128]{3,1,2,0:T(8,128)(2,1)} %get-tuple-element.13) | copy-start | bytes 1572868
  359.5 10.3 %copy-start.1 = (bf16[1,16,128,128]{3,1,2,0:T(8,128)(2,1)S(1)}, bf16[1,16,128,128]{3,1,2,0:T(8,128)(2,1)}, u32[]{:S(2)}) copy-start(bf16[1,16,128,128]{3,1,2,0:T(8,128)(2,1)} %get-tuple-element.14) | copy-start | bytes 1572868
  359.5 11.1 %copy-start = (bf16[1,16,128,128]{3,1,2,0:T(8,128)(2,1)S(1)}, bf16[1,16,128,128]{3,1,2,0:T(8,128)(2,1)}, u32[]{:S(2)}) copy-start(bf16[1,16,128,128]{3,1,2,0:T(8,128)(2,1)} %get-tuple-element.15) | copy-start | bytes 1572868
Sparse Core Ops, SparseCore 0:
  274.0 85.4 all-reduce.2
Sparse Core Ops, SparseCore 1:
  275.9 79.1 all-gather.1
where the time goes:
time: 425 us; the launch traced here: 424 us
  waiting for transfers between devices  254 us (60%)
  local copies, waits for them, and re-layouts  91.6 us (22%)
  matrix products  47.6 us (11%)
  between operations  15.6 us (4%)
  starting transfers between devices  13.9 us (3%)
    all_to_all x1, waiting for transfers between devices, local(): lax.all_to_all(packed, ('row', 'col'), split_axis=0, concat_axis=0, tiled...  183 us
    psum x1, waiting for transfers between devices, from_root(): return lax.psum(kept, axis)  70.7 us
    unnamed x24, local copies, waits for them, and re-layouts  58.6 us
    dot_general x1, matrix products, local(): lax.dot_general(phi_batch, weighted, (((0,), (0,)), ((), ())), preferred_...  15.6 us
    dot_general x1, matrix products, local(): jnp.dot(piece.reshape(local_rows * block_size, width), head_matrix, prefe...  12.6 us
    dot_general x1, matrix products, sum_into_tile(): lax.dot_general(selector.astype(jnp.bfloat16), received, (((0,), (0,)), (...  12 us
    another operation x9, local copies, waits for them, and re-layouts, local(): head_stack = jnp.stack(gathered_rows, axis=0)  10 us
    reshape x1, local copies, waits for them, and re-layouts, local(): partial_sum.reshape(list_length, block_size, list_length, block_size)  9.42 us
  transfers between devices with their start and end apart: 4, of which 2 were waited for; matrix products, arithmetic and copies ran while one was open for 17% of the time, Pallas kernels for 0%

commit v1 on v0

--- a/solution.py
+++ b/solution.py
@@ -1,3 +1,4 @@
+import functools
 import jax
 import jax.numpy as jnp
 from jax import lax
@@ -5,6 +6,37 @@
 
 NB = 8192
 WIN = 16
+
+
+def reach_the_inputs(x0, d0, buf):
+    taken_in = x0.shape
+    return jnp.moveaxis(
+        x0.reshape(*taken_in[:d0], buf, taken_in[d0] // buf, *taken_in[d0 + 1 :]), d0, 0
+    )
+
+
+def _process_state(local_values, at_axis):
+    step_out = list(local_values.shape[1:])
+    step_out[at_axis] *= local_values.shape[0]
+    return jnp.moveaxis(local_values, 0, at_axis).reshape(step_out)
+
+
+def part_marks(field, across, packet, x_part):
+    odd, response = (lax.axis_size(across), lax.axis_index(across))
+    part_next = reach_the_inputs(field, packet, odd)
+    all_blocks = [part_next[response]]
+    for idx in tuple(range(1, odd)):
+        seen_now = part_next[response ^ idx]
+        all_blocks.append(
+            lax.ppermute(
+                seen_now, axis_name=across, perm=[(to_i, to_i ^ idx) for to_i in range(odd)]
+            )
+        )
+    part_next = jnp.stack(all_blocks, 0)[response ^ jnp.arange(odd)]
+    return _process_state(part_next, x_part)
+
+
+report_slots = functools.partial(part_marks, across=("row", "col"), packet=0, x_part=0)
 
 
 def from_root(value, axis, source):
@@ -79,7 +111,7 @@
     packed = packed.reshape(device_count, capacity, block_area)
     slot_labels = slot_labels.reshape(device_count, capacity)
     received, received_labels = (
-        lax.all_to_all(packed, ("row", "col"), split_axis=0, concat_axis=0, tiled=True),
+        report_slots(packed),
         lax.all_to_all(slot_labels, ("row", "col"), split_axis=0, concat_axis=0, tiled=True),
     )
     tile = sum_into_tile(received.reshape(-1, block_area), received_labels.reshape(-1), tile_blocks)

time: 425 us -> 501 us (1.18)
  starting transfers between devices: 13.9 us -> 45.1 us
  local copies, waits for them, and re-layouts: 91.6 us -> 121 us
  waiting for transfers between devices: 254 us -> 270 us
    ppermute x0 -> x15, waiting for transfers between devices: none -> 187 us  [part_marks(): lax.ppermute(seen_now, axis_name=across, perm=[(to_i, to_i ^ idx) for to_...]
    all_to_all x1 -> x0, waiting for transfers between devices: 183 us -> none  [local(): lax.all_to_all(packed, ('row', 'col'), split_axis=0, concat_axis=0, tiled...]
    ppermute x0 -> x15, starting transfers between devices: none -> 39.8 us  [part_marks(): lax.ppermute(seen_now, axis_name=across, perm=[(to_i, to_i ^ idx) for to_...]
    unnamed x24 -> x36, local copies, waits for them, and re-layouts: 58.6 us -> 71.9 us
    gather x0 -> x1, local copies, waits for them, and re-layouts: none -> 8.31 us  [part_marks(): part_next = jnp.stack(all_blocks, 0)[response ^ jnp.arange(odd)]]
    psum x1, waiting for transfers between devices: 70.7 us -> 78.3 us  [from_root(): return lax.psum(kept, axis)]
    all_to_all x1 -> x0, starting transfers between devices: 6.06 us -> none  [local(): lax.all_to_all(packed, ('row', 'col'), split_axis=0, concat_axis=0, tiled...]
  transfers between devices with their start and end apart: 4 -> 18, of which waited for: 2 -> 12; matrix products, arithmetic and copies ran while one was open for 17% -> 9% of each run, Pallas kernels for 0% -> 0%
where the time goes in v1:
time: 501 us; the launch traced here: 499 us
  waiting for transfers between devices  270 us (54%)
  local copies, waits for them, and re-layouts  121 us (24%)
  matrix products  46.5 us (9%)
  starting transfers between devices  45.1 us (9%)
  between operations  15.7 us (3%)
    ppermute x15, waiting for transfers between devices, part_marks(): lax.ppermute(seen_now, axis_name=across, perm=[(to_i, to_i ^ idx) for to_...  187 us
    psum x1, waiting for transfers between devices, from_root(): return lax.psum(kept, axis)  78.3 us
    unnamed x36, local copies, waits for them, and re-layouts  71.9 us
    ppermute x15, starting transfers between devices, part_marks(): lax.ppermute(seen_now, axis_name=across, perm=[(to_i, to_i ^ idx) for to_...  39.8 us
    dot_general x1, matrix products, local(): lax.dot_general(phi_batch, weighted, (((0,), (0,)), ((), ())), preferred_...  15.6 us
    dot_general x1, matrix products, local(): jnp.dot(piece.reshape(local_rows * block_size, width), head_matrix, prefe...  12.6 us
    dot_general x1, matrix products, sum_into_tile(): lax.dot_general(selector.astype(jnp.bfloat16), received, (((0,), (0,)), (...  12 us
    another operation x9, local copies, waits for them, and re-layouts, local(): head_stack = jnp.stack(gathered_rows, axis=0)  11.1 us
  transfers between devices with their start and end apart: 18, of which 12 were waited for; matrix products, arithmetic and copies ran while one was open for 9% of the time, Pallas kernels for 0%

profile of v1, /device:TPU:0, one launch (start us, length us, event | category | flops | bytes accessed | tf_op | source)
XLA Modules:
  0.0 499.2 jit_solution(15266270771601949047)
XLA Ops:
  9.9 15.6 %fusion = bf16[1536,1536]{0,1:T(8,128)(2,1)} fusion(bf16[1,1,2048,1536]{3,2,1,0:T(8,128)(2,1)} %param.4, f32[2048]{0:T(1024)} %bitcast.154), kind=kOutput, calls=%fused_computation.5 | convolution fusion | flops 9675472896 | bytes 11018240 | tf_op jit(solution)/shard_map/dot_general | solution.py:90
  25.5 6.6 %copy.20 = bf16[1536,1536]{1,0:T(8,128)(2,1)} copy(bf16[1536,1536]{0,1:T(8,128)(2,1)} %fusion) | data formatting | bytes 9437184 | tf_op jit(solution)/shard_map/convert_element_type | solution.py:92
  32.1 9.4 %reshape.297 = bf16[12,128,12,128]{3,2,1,0:T(8,128)(2,1)} reshape(bf16[1536,1536]{1,0:T(8,128)(2,1)} %copy.20) | data formatting | bytes 9437184 | tf_op jit(solution)/shard_map/reshape | solution.py:93
  41.5 6.3 %copy.21 = bf16[12,12,128,128]{3,2,1,0:T(8,128)(2,1)} copy(bf16[12,12,128,128]{3,1,2,0:T(8,128)(2,1)} %bitcast.139) | data formatting | bytes 9437184 | tf_op jit(solution)/shard_map/transpose | solution.py:93
  47.8 6.3 %convolution_convert_fusion = bf16[256,16384]{1,0:T(8,128)(2,1)S(1)} fusion(bf16[18,8,128,128]{3,2,1,0:T(8,128)(2,1)} %bitcast.140, s32[144]{0:T(256)S(1)} %multiply_add_fusion), kind=kOutput, calls=%fused_computation.1 | convolution fusion | flops 1212190720 | bytes 13107776 | tf_op jit(solution)/shard_map/dot_general | solution.py:57
  54.1 3.2 dynamic-slice_bitcast_fusion
  57.4 3.0 collective-permute-start
  61.2 4.9 all-to-all-start
  66.3 4.4 collective-permute-start.14
  70.8 1.8 collective-permute-start.12
  72.6 4.5 all-to-all-done
  78.9 0.8 bitcast_dynamic-update-slice_fusion.14
  79.7 67.3 %collective-permute-done.1 = bf16[1,16,16384]{2,1,0:T(8,128)(2,1)S(1)} collective-permute-done((bf16[1,16,16384]{2,1,0:T(8,128)(2,1)}, bf16[1,16,16384]{2,1,0:T(8,128)(2,1)S(1)}, u32[]{:S(2)}, u32[]{:S(2)}) %collective-permute-start.1) | collective-permute-done | bytes 524320 | tf_op jit(solution)/shard_map/ppermute | solution.py:31
  147.0 2.8 collective-permute-start.2
  149.8 0.8 bitcast_dynamic-update-slice_fusion.13
  150.6 12.1 %collective-permute-done.2 = bf16[1,16,16384]{2,1,0:T(8,128)(2,1)S(1)} collective-permute-done((bf16[1,16,16384]{2,1,0:T(8,128)(2,1)}, bf16[1,16,16384]{2,1,0:T(8,128)(2,1)S(1)}, u32[]{:S(2)}, u32[]{:S(2)}) %collective-permute-start.2) | collective-permute-done | bytes 524320 | tf_op jit(solution)/shard_map/ppermute | solution.py:31
  162.8 0.8 bitcast_dynamic-update-slice_fusion.12
  163.6 1.3 collective-permute-done.3
  164.9 9.1 %collective-permute-start.4 = (bf16[1,16,16384]{2,1,0:T(8,128)(2,1)}, bf16[1,16,16384]{2,1,0:T(8,128)(2,1)S(1)}, u32[]{:S(2)}, u32[]{:S(2)}) collective-permute-start(bf16[1,16,16384]{2,1,0:T(8,128)(2,1)} %get-tuple-element.34), channel_id=1, source_target_pairs={{0,5},{1,4},{2,7},{3,6},{4,1},{5,0},{6,3},{7,2},{8,13},{9,12},{10,... | collective-permute-start | bytes 1572872 | tf_op jit(solution)/shard_map/ppermute | solution.py:31
  174.0 0.8 bitcast_dynamic-update-slice_fusion.11
  174.9 11.5 %collective-permute-done.4 = bf16[1,16,16384]{2,1,0:T(8,128)(2,1)S(1)} collective-permute-done((bf16[1,16,16384]{2,1,0:T(8,128)(2,1)}, bf16[1,16,16384]{2,1,0:T(8,128)(2,1)S(1)}, u32[]{:S(2)}, u32[]{:S(2)}) %collective-permute-start.4) | collective-permute-done | bytes 524320 | tf_op jit(solution)/shard_map/ppermute | solution.py:31
  186.3 1.5 collective-permute-start.5
  187.9 0.8 bitcast_dynamic-update-slice_fusion.10
  188.7 23.9 %collective-permute-done.5 = bf16[1,16,16384]{2,1,0:T(8,128)(2,1)S(1)} collective-permute-done((bf16[1,16,16384]{2,1,0:T(8,128)(2,1)}, bf16[1,16,16384]{2,1,0:T(8,128)(2,1)S(1)}, u32[]{:S(2)}, u32[]{:S(2)}) %collective-permute-start.5) | collective-permute-done | bytes 524320 | tf_op jit(solution)/shard_map/ppermute | solution.py:31
  212.6 1.2 collective-permute-start.6
  213.9 0.8 bitcast_dynamic-update-slice_fusion.9
  214.7 14.0 %collective-permute-done.6 = bf16[1,16,16384]{2,1,0:T(8,128)(2,1)S(1)} collective-permute-done((bf16[1,16,16384]{2,1,0:T(8,128)(2,1)}, bf16[1,16,16384]{2,1,0:T(8,128)(2,1)S(1)}, u32[]{:S(2)}, u32[]{:S(2)}) %collective-permute-start.6) | collective-permute-done | bytes 524320 | tf_op jit(solution)/shard_map/ppermute | solution.py:31
  228.7 0.8 bitcast_dynamic-update-slice_fusion.8
  229.5 13.3 %collective-permute-done.7 = bf16[1,16,16384]{2,1,0:T(8,128)(2,1)S(1)} collective-permute-done((bf16[1,16,16384]{2,1,0:T(8,128)(2,1)}, bf16[1,16,16384]{2,1,0:T(8,128)(2,1)S(1)}, u32[]{:S(2)}, u32[]{:S(2)}) %collective-permute-start.7) | collective-permute-done | bytes 524320 | tf_op jit(solution)/shard_map/ppermute | solution.py:31
  242.8 8.4 %collective-permute-start.8 = (bf16[1,16,16384]{2,1,0:T(8,128)(2,1)}, bf16[1,16,16384]{2,1,0:T(8,128)(2,1)S(1)}, u32[]{:S(2)}, u32[]{:S(2)}) collective-permute-start(bf16[1,16,16384]{2,1,0:T(8,128)(2,1)} %get-tuple-element.30), channel_id=1, source_target_pairs={{0,9},{1,8},{2,11},{3,10},{4,13},{5,12},{6,15},{7,14},{8,1},{9,0},... | collective-permute-start | bytes 1572872 | tf_op jit(solution)/shard_map/ppermute | solution.py:31
  251.2 0.8 bitcast_dynamic-update-slice_fusion.7
  252.0 11.0 %collective-permute-done.8 = bf16[1,16,16384]{2,1,0:T(8,128)(2,1)S(1)} collective-permute-done((bf16[1,16,16384]{2,1,0:T(8,128)(2,1)}, bf16[1,16,16384]{2,1,0:T(8,128)(2,1)S(1)}, u32[]{:S(2)}, u32[]{:S(2)}) %collective-permute-start.8) | collective-permute-done | bytes 524320 | tf_op jit(solution)/shard_map/ppermute | solution.py:31
  263.0 3.6 collective-permute-start.9
  267.5 21.4 %collective-permute-done.9 = bf16[1,16,16384]{2,1,0:T(8,128)(2,1)S(1)} collective-permute-done((bf16[1,16,16384]{2,1,0:T(8,128)(2,1)S(1)}, bf16[1,16,16384]{2,1,0:T(8,128)(2,1)S(1)}, u32[]{:S(2)}, u32[]{:S(2)}) %collective-permute-start.9) | collective-permute-done | bytes 524320 | tf_op jit(solution)/shard_map/ppermute | solution.py:31
  288.8 3.4 collective-permute-start.10
  293.1 10.9 %collective-permute-done.10 = bf16[1,16,16384]{2,1,0:T(8,128)(2,1)S(1)} collective-permute-done((bf16[1,16,16384]{2,1,0:T(8,128)(2,1)S(1)}, bf16[1,16,16384]{2,1,0:T(8,128)(2,1)S(1)}, u32[]{:S(2)}, u32[]{:S(2)}) %collective-permute-start.10) | collective-permute-done | bytes 524320 | tf_op jit(solution)/shard_map/ppermute | solution.py:31
  304.0 0.8 bitcast_dynamic-update-slice_fusion.4
  304.9 0.8 bitcast_dynamic-update-slice_fusion.3
  305.7 0.8 bitcast_dynamic-update-slice_fusion.2
  306.5 0.8 bitcast_dynamic-update-slice_fusion.1
  307.3 0.8 bitcast_dynamic-update-slice_fusion
  308.2 8.3 %gather_fusion = bf16[16,16,16384]{2,1,0:T(8,128)(2,1)} fusion(bf16[16,16,16384]{2,1,0:T(8,128)(2,1)} %bitcast.142, s32[1024]{0:T(1024)S(1)} %pad_clamp_fusion), kind=kCustom, calls=%fused_computation | custom fusion | bytes 16777280 | tf_op jit(solution)/shard_map/gather | solution.py:35
  316.5 12.0 %fusion.18 = (bf16[256,16384]{1,0:T(8,128)(2,1)S(1)}, f32[256,16384]{1,0:T(8,128)}) fusion(bf16[256,16384]{1,0:T(8,128)(2,1)} %bitcast.138, s32[256]{0:T(256)S(1)} %eq.66), kind=kOutput, calls=%fused_computation.92 | convolution fusion | flops 2151743488 | bytes 33555456 | tf_op jit(solution)/shard_map/dot_general | solution.py:66
  328.9 1.1 copy.29
  330.1 1.2 copy.23
  331.4 1.1 copy.24
  332.6 1.1 copy.27
  333.8 1.1 copy.28
  335.1 1.1 copy.26
  336.3 1.2 copy.22
  337.6 1.2 copy.25
  339.3 14.2 %copy.33 = f32[32,8,128,128]{3,2,1,0:T(8,128)} copy(f32[32,8,128,128]{3,1,2,0:T(8,128)} %bitcast.135) | data formatting | bytes 33554432
  353.5 78.3 %all-reduce.3.cloned.1.call-done = (bf16[1,16,128,128]{3,1,2,0:T(8,128)(2,1)}, bf16[1,16,128,128]{3,1,2,0:T(8,128)(2,1)}, bf16[1,16,128,128]{3,1,2,0:T(8,128)(2,...) async-done(((bf16[1,16,128,128]{3,1,2,0:T(8,128)(2,1)}, ...) | async-done | bytes 4194320 | tf_op jit(solution)/shard_map/psum | solution.py:44
  431.8 1.9 constant_dynamic-update-slice_fusion.7
  433.7 1.9 constant_dynamic-update-slice_fusion.6
  435.6 1.9 constant_dynamic-update-slice_fusion.5
  437.4 1.9 constant_dynamic-update-slice_fusion.4
  439.3 1.9 constant_dynamic-update-slice_fusion.3
  441.2 1.9 constant_dynamic-update-slice_fusion.2
  443.0 1.9 constant_dynamic-update-slice_fusion.1
  444.9 1.9 constant_dynamic-update-slice_fusion
  446.8 12.6 %convolution_bitcast_fusion = f32[256,8,16,128]{3,1,2,0:T(8,128)S(1)} fusion(bf16[2048,1024]{1,0:T(8,128)(2,1)} %bitcast.153, bf16[128,8,16,128]{3,2,1,0:T(8,128)(2,1)} %bitcast.76), kind=kOutput, calls=%fused_computation.3 | convolution fusion | flops 8589934592 | bytes 25165824 | tf_op jit(solution)/shard_map/dot_general | solution.py:132
  459.4 7.5 %copy.43 = f32[256,8,16,128]{3,2,1,0:T(8,128)} copy(f32[256,8,16,128]{3,1,2,0:T(8,128)S(1)} %convolution_bitcast_fusion) | data formatting | bytes 33554432
  466.9 24.9 %copy.31 = f32[16,1,128,16,1,128]{5,4,3,2,1,0:T(1,128)} copy(f32[16,1,128,16,1,128]{2,0,5,3,4,1:T(8,128)} %bitcast.136) | data formatting | bytes 33554432
  (45 shorter events, 7.9 us)
Async XLA Ops:
  57.4 21.2 %collective-permute-start = (bf16[1,16,16384]{2,1,0:T(8,128)(2,1)}, bf16[1,16,16384]{2,1,0:T(8,128)(2,1)S(1)}, u32[]{:S(2)}, u32[]{:S(2)}) collective-permute-start(bf16[1,16,16384]{2,1,0:T(8,128)(2,1)} %get-tuple-element.38), channel_id=1, source_target_pairs={{0,1},{1,0},{2,3},{3,2},{4,5},{5,4},{6,7},{7,6},{8,9},{9,8},{10,11... | collective-permute-start | bytes 1572872 | tf_op jit(solution)/shard_map/ppermute | solution.py:31
  61.2 15.9 %all-to-all-start = ((s32[16,1,16]{2,1,0:T(1,128)}), s32[16,1,16]{2,1,0:T(1,128)S(1)}, u32[]{:S(2)}, u32[]{:S(2)}) async-start(s32[16,1,16]{2,1,0:T(1,128)} %sub.19), calls=%async_computation | async-start | bytes 16384 | tf_op jit(solution)/shard_map/all_to_all | solution.py:115
  66.1 365.7 %all-reduce.3.cloned.1.call-start = ((), (), s32[]{:S(2)}) async-start(), calls=%async_computation.2 | async-start | bytes 8388608 | tf_op jit(solution)/shard_map/psum | solution.py:44
  66.3 241.0 %collective-permute-start.14 = (bf16[1,16,16384]{2,1,0:T(8,128)(2,1)S(1)}, bf16[1,16,16384]{2,1,0:T(8,128)(2,1)S(1)}, u32[]{:S(2)}, u32[]{:S(2)}) collective-permute-start(bf16[1,16,16384]{2,1,0:T(8,128)(2,1)S(1)} %get-tuple-element.24), channel_id=1, source_target_pairs={{0,15},{1,14},{2,13},{3,12},{4,11},{5,10},{6,9},{7,8},{8,7},{9,6},... | collective-permute-start | bytes 1572872 | tf_op jit(solution)/shard_map/ppermute | solution.py:31
  70.8 235.7 %collective-permute-start.13 = (bf16[1,16,16384]{2,1,0:T(8,128)(2,1)}, bf16[1,16,16384]{2,1,0:T(8,128)(2,1)S(1)}, u32[]{:S(2)}, u32[]{:S(2)}) collective-permute-start(bf16[1,16,16384]{2,1,0:T(8,128)(2,1)} %get-tuple-element.25), channel_id=1, source_target_pairs={{0,14},{1,15},{2,12},{3,13},{4,10},{5,11},{6,8},{7,9},{8,6},{9,7},... | collective-permute-start | bytes 1572872 | tf_op jit(solution)/shard_map/ppermute | solution.py:31
  70.8 234.9 %collective-permute-start.12 = (bf16[1,16,16384]{2,1,0:T(8,128)(2,1)}, bf16[1,16,16384]{2,1,0:T(8,128)(2,1)S(1)}, u32[]{:S(2)}, u32[]{:S(2)}) collective-permute-start(bf16[1,16,16384]{2,1,0:T(8,128)(2,1)} %get-tuple-element.26), channel_id=1, source_target_pairs={{0,13},{1,12},{2,15},{3,14},{4,9},{5,8},{6,11},{7,10},{8,5},{9,4},... | collective-permute-start | bytes 1572872 | tf_op jit(solution)/shard_map/ppermute | solution.py:31
  72.5 232.3 %collective-permute-start.11 = (bf16[1,16,16384]{2,1,0:T(8,128)(2,1)}, bf16[1,16,16384]{2,1,0:T(8,128)(2,1)S(1)}, u32[]{:S(2)}, u32[]{:S(2)}) collective-permute-start(bf16[1,16,16384]{2,1,0:T(8,128)(2,1)} %get-tuple-element.27), channel_id=1, source_target_pairs={{0,12},{1,13},{2,14},{3,15},{4,8},{5,9},{6,10},{7,11},{8,4},{9,5},... | collective-permute-start | bytes 1572872 | tf_op jit(solution)/shard_map/ppermute | solution.py:31
  78.5 184.5 %copy-start.1 = (bf16[1,16,16384]{2,1,0:T(8,128)(2,1)S(1)}, bf16[1,16,16384]{2,1,0:T(8,128)(2,1)}, u32[]{:S(2)}) copy-start(bf16[1,16,16384]{2,1,0:T(8,128)(2,1)} %get-tuple-element.29) | copy-start | bytes 1572868
  78.5 210.3 %copy-start = (bf16[1,16,16384]{2,1,0:T(8,128)(2,1)S(1)}, bf16[1,16,16384]{2,1,0:T(8,128)(2,1)}, u32[]{:S(2)}) copy-start(bf16[1,16,16384]{2,1,0:T(8,128)(2,1)} %get-tuple-element.28) | copy-start | bytes 1572868
  78.5 68.5 %collective-permute-start.1 = (bf16[1,16,16384]{2,1,0:T(8,128)(2,1)}, bf16[1,16,16384]{2,1,0:T(8,128)(2,1)S(1)}, u32[]{:S(2)}, u32[]{:S(2)}) collective-permute-start(bf16[1,16,16384]{2,1,0:T(8,128)(2,1)} %get-tuple-element.37), channel_id=1, source_target_pairs={{0,2},{1,3},{2,0},{3,1},{4,6},{5,7},{6,4},{7,5},{8,10},{9,11},{10,... | collective-permute-start | bytes 1572872 | tf_op jit(solution)/shard_map/ppermute | solution.py:31
  147.0 15.7 %collective-permute-start.2 = (bf16[1,16,16384]{2,1,0:T(8,128)(2,1)}, bf16[1,16,16384]{2,1,0:T(8,128)(2,1)S(1)}, u32[]{:S(2)}, u32[]{:S(2)}) collective-permute-start(bf16[1,16,16384]{2,1,0:T(8,128)(2,1)} %get-tuple-element.36), channel_id=1, source_target_pairs={{0,3},{1,2},{2,1},{3,0},{4,7},{5,6},{6,5},{7,4},{8,11},{9,10},{10,... | collective-permute-start | bytes 1572872 | tf_op jit(solution)/shard_map/ppermute | solution.py:31
  162.8 2.1 collective-permute-start.3
  164.9 21.4 %collective-permute-start.4 = (bf16[1,16,16384]{2,1,0:T(8,128)(2,1)}, bf16[1,16,16384]{2,1,0:T(8,128)(2,1)S(1)}, u32[]{:S(2)}, u32[]{:S(2)}) collective-permute-start(bf16[1,16,16384]{2,1,0:T(8,128)(2,1)} %get-tuple-element.34), channel_id=1, source_target_pairs={{0,5},{1,4},{2,7},{3,6},{4,1},{5,0},{6,3},{7,2},{8,13},{9,12},{10,... | collective-permute-start | bytes 1572872 | tf_op jit(solution)/shard_map/ppermute | solution.py:31
  186.3 26.3 %collective-permute-start.5 = (bf16[1,16,16384]{2,1,0:T(8,128)(2,1)}, bf16[1,16,16384]{2,1,0:T(8,128)(2,1)S(1)}, u32[]{:S(2)}, u32[]{:S(2)}) collective-permute-start(bf16[1,16,16384]{2,1,0:T(8,128)(2,1)} %get-tuple-element.33), channel_id=1, source_target_pairs={{0,6},{1,7},{2,4},{3,5},{4,2},{5,3},{6,0},{7,1},{8,14},{9,15},{10,... | collective-permute-start | bytes 1572872 | tf_op jit(solution)/shard_map/ppermute | solution.py:31
  212.6 16.0 %collective-permute-start.6 = (bf16[1,16,16384]{2,1,0:T(8,128)(2,1)}, bf16[1,16,16384]{2,1,0:T(8,128)(2,1)S(1)}, u32[]{:S(2)}, u32[]{:S(2)}) collective-permute-start(bf16[1,16,16384]{2,1,0:T(8,128)(2,1)} %get-tuple-element.32), channel_id=1, source_target_pairs={{0,7},{1,6},{2,5},{3,4},{4,3},{5,2},{6,1},{7,0},{8,15},{9,14},{10,... | collective-permute-start | bytes 1572872 | tf_op jit(solution)/shard_map/ppermute | solution.py:31
  228.7 14.2 %collective-permute-start.7 = (bf16[1,16,16384]{2,1,0:T(8,128)(2,1)}, bf16[1,16,16384]{2,1,0:T(8,128)(2,1)S(1)}, u32[]{:S(2)}, u32[]{:S(2)}) collective-permute-start(bf16[1,16,16384]{2,1,0:T(8,128)(2,1)} %get-tuple-element.31), channel_id=1, source_target_pairs={{0,8},{1,9},{2,10},{3,11},{4,12},{5,13},{6,14},{7,15},{8,0},{9,1},... | collective-permute-start | bytes 1572872 | tf_op jit(solution)/shard_map/ppermute | solution.py:31
  242.8 20.2 %collective-permute-start.8 = (bf16[1,16,16384]{2,1,0:T(8,128)(2,1)}, bf16[1,16,16384]{2,1,0:T(8,128)(2,1)S(1)}, u32[]{:S(2)}, u32[]{:S(2)}) collective-permute-start(bf16[1,16,16384]{2,1,0:T(8,128)(2,1)} %get-tuple-element.30), channel_id=1, source_target_pairs={{0,9},{1,8},{2,11},{3,10},{4,13},{5,12},{6,15},{7,14},{8,1},{9,0},... | collective-permute-start | bytes 1572872 | tf_op jit(solution)/shard_map/ppermute | solution.py:31
  263.0 25.8 %collective-permute-start.9 = (bf16[1,16,16384]{2,1,0:T(8,128)(2,1)S(1)}, bf16[1,16,16384]{2,1,0:T(8,128)(2,1)S(1)}, u32[]{:S(2)}, u32[]{:S(2)}) collective-permute-start(bf16[1,16,16384]{2,1,0:T(8,128)(2,1)S(1)} %copy-done.1), channel_id=1, source_target_pairs={{0,10},{1,11},{2,8},{3,9},{4,14},{5,15},{6,12},{7,13},{8,2},{9,3},... | collective-permute-start | bytes 1572872 | tf_op jit(solution)/shard_map/ppermute | solution.py:31
  288.8 15.2 %collective-permute-start.10 = (bf16[1,16,16384]{2,1,0:T(8,128)(2,1)S(1)}, bf16[1,16,16384]{2,1,0:T(8,128)(2,1)S(1)}, u32[]{:S(2)}, u32[]{:S(2)}) collective-permute-start(bf16[1,16,16384]{2,1,0:T(8,128)(2,1)S(1)} %copy-done), channel_id=1, source_target_pairs={{0,11},{1,10},{2,9},{3,8},{4,15},{5,14},{6,13},{7,12},{8,3},{9,2},... | collective-permute-start | bytes 1572872 | tf_op jit(solution)/shard_map/ppermute | solution.py:31
  338.8 108.0 %all-gather.2.cloned.1.call-start = ((), (), s32[]{:S(2)}) async-start(), calls=%async_computation.1 | async-start | bytes 5242880 | tf_op jit(solution)/shard_map/all_gather | solution.py:130
Sparse Core Ops, SparseCore 0:
  338.9 92.9 all-reduce.2
Sparse Core Ops, SparseCore 1:
  340.8 86.5 all-gather.1
